TPU v7x, 128 devices: a whole 4x4x4 slice. The times are simulated.
128 devices in a mesh: mp: 2 (over core), tile: 64 (over y, z, x).
Axes of the slice: x: 4, y: 4, z: 4, core: 2. Of those that a mesh axis runs over, the one named last changes fastest.
Arguments:
- tracers: float32 [2, 4, 64, 1024, 512], P('mp', None, None, 'tile'), may hold values from -6 to 6
- diffusivity: float32 [2, 63, 1024, 512], P('mp', None, 'tile'), may hold values from 0.05 to 60
- conductance: float32 [2, 1024, 512], P('mp', 'tile'), may hold values from 0.2 to 4
- face_velocity: float32 [2, 64, 1024, 512], P('mp', None, 'tile'), may hold values from -0.3 to 0.3
- partner: int32 [2, 2, 1024, 512], P('mp', None, 'tile'), may hold values from 0 to 1023, as said below
- weight: int32 [2, 2, 1024, 512], P('mp', None, 'tile'), may hold values from 0 to 15, as said below
- sea_mask: int32 [1024, 512], P('tile'), may hold values from 0 to 1, as said below
Outputs:
- tracers_out: float32 [2, 4, 64, 1024, 512], P('mp', None, None, 'tile')
- surface_inflow: float32 [2, 4, 1024, 512], P('mp', None, 'tile')
Inputs may be any that keep to these rules, and one draw needn't show every extreme that they name: `partner`: entry [m, k, x, y] names a column of the other component in the same row y that intersects column (x, y) of component m, at most 9 cells from x along the periodic X direction; each intersection is listed on both sides with the same weight. `weight`: intersection area in units of 1 / 16 of a cell; 0 exactly where the ocean column of the intersection is land. `sea_mask`: 1 marks an ocean column, 0 land.
All inputs are finite; a program needn't handle non-finite values.
Results may differ from a plain program's by a relative error of at most 0.00002.
Values sent between devices are 32-bit elements; how exact they have to be, the bound alone decides.
A program may use at most 192 MiB of HBM per device.

v0:
```python
import functools

import jax
import jax.numpy as jnp
from jax import lax
from jax.experimental import pallas as pl
from jax.experimental.pallas import tpu as pltpu
from jax.sharding import PartitionSpec as P

STEPS = 4
QUANT = 16
CHUNK = 8
REACH = 9

diffusion_nu = 0.12
MESH = pl.DeviceIdType.MESH


def kernel(
    count,
    tracers,
    diffusivity,
    conductance,
    velocity,
    partner,
    weight,
    sea_mask,
    out,
    inflow_out,
    q,
    lower,
    ratio,
    inverse,
    speed,
    keep,
    east,
    west,
    from_left,
    from_right,
    speed_left,
    mask_own,
    mask_left,
    mask_right,
    terms,
    wide,
    partner_own,
    weight_own,
    inflow,
    load_sem,
    tracer_sem,
    store_sem,
    misc_send,
    misc_recv,
    edge_send,
    edge_recv,
):
    _, trac, lev, width, rows = q.shape
    chunks = lev // CHUNK
    component = lax.axis_index("mp")
    tile = lax.axis_index("tile")
    other = 1 - component
    right = lax.rem(tile + 1, count)
    left = lax.rem(tile + count - 1, count)
    half = width // 2

    def chunk_load(c):
        part = pl.ds(c * CHUNK, CHUNK)
        return pltpu.make_async_copy(tracers.at[0, :, part], q.at[0, :, part], tracer_sem.at[c])

    def chunk_store(c):
        part = pl.ds(c * CHUNK, CHUNK)
        return pltpu.make_async_copy(q.at[0, :, part], out.at[0, :, part], store_sem.at[c])

    loads = [
        pltpu.make_async_copy(source, target, load_sem.at[i])
        for i, (source, target) in enumerate(
            [
                (diffusivity.at[0], lower.at[pl.ds(0, lev - 1)]),
                (conductance.at[0], terms.at[trac + 1]),
                (sea_mask, mask_own),
                (velocity.at[0], speed),
                (partner.at[0], partner_own),
                (weight.at[0], weight_own),
            ]
        )
    ]
    loads[0].start()
    for c in range(chunks):
        chunk_load(c).start()
    for load in loads[1:]:
        load.start()

    barrier = pltpu.get_barrier_semaphore()
    peers = [(component, left), (component, right), (other, tile), (other, left), (other, right)]
    for peer in peers:
        pl.semaphore_signal(barrier, inc=1, device_id=peer, device_id_type=MESH)
    pl.semaphore_wait(barrier, len(peers))

    def send(index, source, target, peer):
        return pltpu.make_async_remote_copy(
            src_ref=source,
            dst_ref=target,
            send_sem=misc_send.at[index],
            recv_sem=misc_recv.at[index],
            device_id=peer,
            device_id_type=MESH,
        )

    early = [
        send(0, velocity.at[0, :, width - 1], speed_left, (component, right)),
        send(1, sea_mask.at[pl.ds(half, half)], mask_left, (component, right)),
        send(2, sea_mask.at[pl.ds(0, half)], mask_right, (component, left)),
    ]
    exchange = [
        send(3, terms, wide.at[:, pl.ds(width, width)], (other, tile)),
        send(4, terms.at[:, pl.ds(half, half)], wide.at[:, pl.ds(half, half)], (other, right)),
        send(5, terms.at[:, half - 1], wide.at[:, half - 1], (other, right)),
        send(6, terms.at[:, pl.ds(0, half)], wide.at[:, pl.ds(2 * width, half)], (other, left)),
        send(7, terms.at[:, half], wide.at[:, 2 * width + half], (other, left)),
    ]
    for copy in early:
        copy.start()

    def edges(s, c):
        part = pl.ds(c * CHUNK, CHUNK)
        field = lax.rem(s, 2)
        return [
            pltpu.make_async_remote_copy(
                src_ref=q.at[field, :, part, column],
                dst_ref=target.at[s, c],
                send_sem=edge_send.at[side, s, c],
                recv_sem=edge_recv.at[side, s, c],
                device_id=(component, peer),
                device_id_type=MESH,
            )
            for side, (column, target, peer) in enumerate(
                [(width - 1, from_left, right), (0, from_right, left)]
            )
        ]

    loads[0].wait()
    zero = jnp.zeros((width, rows), jnp.float32)
    lower[lev - 1] = zero

    def factor(l, carry):
        low, ratio_prev = carry
        high = lower[l]
        inv = 1.0 / (1.0 + low + high - low * ratio_prev)
        ratio_now = high * inv
        inverse[l] = inv
        lower[l] = low * inv
        ratio[l] = ratio_now
        return high, ratio_now

    lax.fori_loop(0, lev, factor, (zero, zero))
    slope = inverse[lev - 1]
    ratio[lev - 1] = slope

    def down_chunk(c, carry):
        chunk_load(c).wait()

        def down(k, partial):
            l = c * CHUNK + k
            low = lower[l]
            inv = inverse[l]
            now = tuple(q[0, t, l] * inv + low * partial[t] for t in range(trac))
            for t in range(trac):
                q[0, t, l] = now[t]
            return now

        return lax.fori_loop(0, CHUNK, down, carry)

    finals = lax.fori_loop(0, chunks, down_chunk, (zero,) * trac)
    for t in range(trac):
        terms[t] = finals[t]
    terms[trac] = slope
    loads[1].wait()
    for copy in exchange:
        copy.start()

    for load in loads[2:]:
        load.wait()
    for copy in early:
        copy.wait_recv()
    row = lax.broadcasted_iota(jnp.int32, (width, rows), 0)
    lane = lax.broadcasted_iota(jnp.int32, (width, rows), 1)
    first = row == 0
    last = row == width - 1

    def openness_of(mask):
        return jnp.where(component == 1, mask.astype(jnp.float32), jnp.ones(mask.shape, jnp.float32))

    openness = openness_of(mask_own[...])
    open_right = openness_of(mask_right[pl.ds(0, 1), :])
    open_left = openness_of(mask_left[pl.ds(half - 1, 1), :])
    open_east = openness * jnp.where(last, open_right, pltpu.roll(openness, width - 1, 0))
    open_west = openness * jnp.where(first, open_left, pltpu.roll(openness, 1, 0))
    north = jnp.where(lane == rows - 1, 0.0, diffusion_nu * openness * pltpu.roll(openness, rows - 1, 1))
    south = jnp.where(lane == 0, 0.0, diffusion_nu * openness * pltpu.roll(openness, 1, 1))

    def coefficients(l, _):
        here = speed[l]
        before = jnp.where(first, speed_left[pl.ds(l, 1), :], pltpu.roll(here, 1, 0))
        keep[l] = (
            1.0
            - north
            - south
            - open_east * (jnp.maximum(here, 0.0) + diffusion_nu)
            + open_west * (jnp.minimum(before, 0.0) - diffusion_nu)
        )
        east[l] = open_east * (diffusion_nu - jnp.minimum(here, 0.0))
        west[l] = open_west * (jnp.maximum(before, 0.0) + diffusion_nu)
        return 0

    lax.fori_loop(0, lev, coefficients, 0)

    for copy in exchange:
        copy.wait_recv()
    columns = count * width
    lanes = 128

    def surface(j, _):
        part = pl.ds(pl.multiple_of(j * lanes, lanes), lanes)
        for h in range(2):
            own_rows = pl.ds(h * half, half)
            place = tile * width + h * half + lax.broadcasted_iota(jnp.int32, (half, lanes), 0)
            own = [terms[ch, own_rows, part] for ch in range(trac + 2)]
            total = [jnp.zeros((half, lanes), jnp.float32) for _ in range(trac)]
            distance = [
                lax.rem(partner_own[k, own_rows, part] - place + (REACH + columns), columns)
                for k in range(2)
            ]
            peer = [[jnp.zeros((half, lanes), jnp.float32)] * (trac + 2) for k in range(2)]
            for offset in range(2 * REACH + 1):
                begin = width - REACH + offset + h * half
                hit = [distance[k] == offset for k in range(2)]
                for ch in range(trac + 2):
                    window = wide[ch, pl.ds(begin, half), part]
                    for k in range(2):
                        peer[k][ch] = jnp.where(hit[k], window, peer[k][ch])
            for k in range(2):
                series = own[trac + 1] * peer[k][trac + 1] / (own[trac + 1] + peer[k][trac + 1])
                scale = (
                    weight_own[k, own_rows, part].astype(jnp.float32)
                    * series
                    / (1.0 + series * (own[trac] + peer[k][trac]))
                )
                for t in range(trac):
                    total[t] = total[t] + scale * (own[t] - peer[k][t])
            for t in range(trac):
                inflow[t, own_rows, part] = total[t] * (-1.0 / QUANT)
        return 0

    lax.fori_loop(0, rows // lanes, surface, 0)
    store_inflow = pltpu.make_async_copy(inflow, inflow_out.at[0], load_sem.at[0])
    store_inflow.start()

    def up_chunk(i, carry):
        c = chunks - 1 - i

        def up(k, above):
            l = c * CHUNK + CHUNK - 1 - k
            slant = ratio[l]
            now = tuple(q[0, t, l] + slant * above[t] for t in range(trac))
            for t in range(trac):
                q[0, t, l] = now[t]
            return now

        carry = lax.fori_loop(0, CHUNK, up, carry)
        for copy in edges(0, c):
            copy.start()
        return carry

    lax.fori_loop(0, chunks, up_chunk, tuple(inflow[t] for t in range(trac)))

    def unit(i, _):
        s = i // chunks
        c = chunks - 1 - lax.rem(i, chunks)
        field = lax.rem(s, 2)

        @pl.when(s > 0)
        def _():
            for copy in edges(s - 1, c):
                copy.wait_send()

        for copy in edges(s, c):
            copy.wait_recv()

        def level(k, _):
            l = c * CHUNK + k
            keep_l = keep[l]
            east_l = east[l]
            west_l = west[l]
            for t in range(trac):
                here = q[field, t, l]
                after = jnp.where(last, from_right[s, c, t, pl.ds(k, 1), :], pltpu.roll(here, width - 1, 0))
                before = jnp.where(first, from_left[s, c, t, pl.ds(k, 1), :], pltpu.roll(here, 1, 0))
                q[1 - field, t, l] = (
                    keep_l * here
                    + east_l * after
                    + west_l * before
                    + north * pltpu.roll(here, rows - 1, 1)
                    + south * pltpu.roll(here, 1, 1)
                )
            return 0

        lax.fori_loop(0, CHUNK, level, 0)

        @pl.when(s < STEPS - 1)
        def _():
            for copy in edges(s + 1, c):
                copy.start()

        @pl.when(s == STEPS - 1)
        def _():
            chunk_store(c).start()

        return 0

    lax.fori_loop(0, STEPS * chunks, unit, 0)

    for c in range(chunks):
        for copy in edges(STEPS - 1, c):
            copy.wait_send()
        chunk_store(c).wait()
    for copy in early + exchange:
        copy.wait_send()
    store_inflow.wait()


def per_device(count, tracers, diffusivity, conductance, face_velocity, partner, weight, sea_mask):
    _, trac, lev, width, rows = tracers.shape
    chunks = lev // CHUNK
    full = (lev, width, rows)
    flat = (width, rows)
    anywhere = pl.BlockSpec(memory_space=pl.ANY)
    edge = (STEPS, chunks, trac, CHUNK, rows)
    dma = pltpu.SemaphoreType.DMA
    real = jnp.float32
    return pl.pallas_call(
        functools.partial(kernel, count),
        out_shape=(
            jax.ShapeDtypeStruct(tracers.shape, real),
            jax.ShapeDtypeStruct((1, trac, width, rows), real),
        ),
        in_specs=[anywhere] * 7,
        out_specs=(anywhere, anywhere),
        scratch_shapes=[
            pltpu.VMEM((2, trac) + full, real),
            pltpu.VMEM(full, real),
            pltpu.VMEM(full, real),
            pltpu.VMEM(full, real),
            pltpu.VMEM(full, real),
            pltpu.VMEM(full, real),
            pltpu.VMEM(full, real),
            pltpu.VMEM(full, real),
            pltpu.VMEM(edge, real),
            pltpu.VMEM(edge, real),
            pltpu.VMEM((lev, rows), real),
            pltpu.VMEM(flat, jnp.int32),
            pltpu.VMEM((width // 2, rows), jnp.int32),
            pltpu.VMEM((width // 2, rows), jnp.int32),
            pltpu.VMEM((trac + 2,) + flat, real),
            pltpu.VMEM((trac + 2, 3 * width, rows), real),
            pltpu.VMEM((2,) + flat, jnp.int32),
            pltpu.VMEM((2,) + flat, jnp.int32),
            pltpu.VMEM((trac,) + flat, real),
            dma((6,)),
            dma((chunks,)),
            dma((chunks,)),
            dma((8,)),
            dma((8,)),
            dma((2, STEPS, chunks)),
            dma((2, STEPS, chunks)),
        ],
        compiler_params=pltpu.CompilerParams(
            collective_id=0, has_side_effects=True, vmem_limit_bytes=56 * 1024 * 1024
        ),
        name="coupled_step",
    )(tracers, diffusivity, conductance, face_velocity, partner, weight, sea_mask)


def solution(mesh):
    in_specs = (
        P("mp", None, None, "tile", None),
        P("mp", None, "tile", None),
        P("mp", "tile", None),
        P("mp", None, "tile", None),
        P("mp", None, "tile", None),
        P("mp", None, "tile", None),
        P("tile", None),
    )
    out_specs = (P("mp", None, None, "tile", None), P("mp", None, "tile", None))
    return jax.shard_map(
        functools.partial(per_device, mesh.shape["tile"]),
        mesh=mesh,
        in_specs=in_specs,
        out_specs=out_specs,
        check_vma=False,
    )
```

profile of v0, /device:TPU:0, one launch (start us, length us, event | category | flops | bytes accessed | tf_op | source)
XLA Modules:
  0.0 128.7 jit_solution(14817931764169120574)
XLA Ops:
  0.6 118.6 %coupled_step.1 = (f32[1,4,64,16,512]{4,3,2,1,0:T(8,128)}, f32[1,4,16,512]{3,2,1,0:T(8,128)}) custom-call(f32[1,4,64,16,512]{4,3,2,1,0:T(8,128)} %tracers.1, f32[1,63,16,512]{3,2,1,0:T(8,128)} %diffusivity.1, f32[1,16,512]{2,1,0:T(8,128)} %conductance.1, f32[1,64,16,512]{3,2,1,0:T(8,128)} %velocity.1, s32[1,2,16,512]{3,2,1,0:T(8,128)} %partner.1, ...), custom_call_target="tpu_custom_call" | custom-call | tf_op jit(solution)/shard_map/coupled_step/pallas_call | solution.py:340
  119.3 0.0 copy-start
  119.3 8.7 %copy.11 = f32[1,4,64,16,512]{4,3,2,1,0:T(8,128)} copy(f32[1,4,64,16,512]{4,3,2,1,0:T(8,128)} %get-tuple-element.4) | data formatting | bytes 16777216
  128.0 0.0 copy-done
  128.0 0.7 copy.12
Async XLA Ops:
  119.3 8.7 %copy-start = (f32[1,4,16,512]{3,2,1,0:T(8,128)S(1)}, f32[1,4,16,512]{3,2,1,0:T(8,128)}, u32[]{:S(2)}) copy-start(f32[1,4,16,512]{3,2,1,0:T(8,128)} %get-tuple-element.5) | copy-start | bytes 393220
where the time goes:
time: 129 us
  Pallas kernels  119 us (92%)
  local copies, waits for them, and re-layouts  9.39 us (7%)
    pallas_call x1, Pallas kernels, per_device(): pl.pallas_call(functools.partial(kernel, count), out_shape=(jax.ShapeDtyp...  119 us
    unnamed x4, local copies, waits for them, and re-layouts  9.39 us

commit v1 on v0

--- a/solution.py
+++ b/solution.py
@@ -27,7 +27,7 @@
     sea_mask,
     out,
     inflow_out,
-    q,
+    spare,
     lower,
     ratio,
     inverse,
@@ -45,16 +45,17 @@
     wide,
     partner_own,
     weight_own,
-    inflow,
     load_sem,
     tracer_sem,
-    store_sem,
     misc_send,
     misc_recv,
     edge_send,
     edge_recv,
 ):
-    _, trac, lev, width, rows = q.shape
+    _, trac, lev, width, rows = out.shape
+    field = out.at[0]
+    inflow = inflow_out.at[0]
+    fields = (field, spare)
     chunks = lev // CHUNK
     component = lax.axis_index("mp")
     tile = lax.axis_index("tile")
@@ -65,11 +66,7 @@
 
     def chunk_load(c):
         part = pl.ds(c * CHUNK, CHUNK)
-        return pltpu.make_async_copy(tracers.at[0, :, part], q.at[0, :, part], tracer_sem.at[c])
-
-    def chunk_store(c):
-        part = pl.ds(c * CHUNK, CHUNK)
-        return pltpu.make_async_copy(q.at[0, :, part], out.at[0, :, part], store_sem.at[c])
+        return pltpu.make_async_copy(tracers.at[0, :, part], field.at[:, part], tracer_sem.at[c])
 
     loads = [
         pltpu.make_async_copy(source, target, load_sem.at[i])
@@ -123,10 +120,9 @@
 
     def edges(s, c):
         part = pl.ds(c * CHUNK, CHUNK)
-        field = lax.rem(s, 2)
         return [
             pltpu.make_async_remote_copy(
-                src_ref=q.at[field, :, part, column],
+                src_ref=fields[s % 2].at[:, part, column],
                 dst_ref=target.at[s, c],
                 send_sem=edge_send.at[side, s, c],
                 recv_sem=edge_recv.at[side, s, c],
@@ -163,9 +159,9 @@
             l = c * CHUNK + k
             low = lower[l]
             inv = inverse[l]
-            now = tuple(q[0, t, l] * inv + low * partial[t] for t in range(trac))
+            now = tuple(field[t, l] * inv + low * partial[t] for t in range(trac))
             for t in range(trac):
-                q[0, t, l] = now[t]
+                field[t, l] = now[t]
             return now
 
         return lax.fori_loop(0, CHUNK, down, carry)
@@ -252,8 +248,6 @@
         return 0
 
     lax.fori_loop(0, rows // lanes, surface, 0)
-    store_inflow = pltpu.make_async_copy(inflow, inflow_out.at[0], load_sem.at[0])
-    store_inflow.start()
 
     def up_chunk(i, carry):
         c = chunks - 1 - i
@@ -261,9 +255,9 @@
         def up(k, above):
             l = c * CHUNK + CHUNK - 1 - k
             slant = ratio[l]
-            now = tuple(q[0, t, l] + slant * above[t] for t in range(trac))
+            now = tuple(field[t, l] + slant * above[t] for t in range(trac))
             for t in range(trac):
-                q[0, t, l] = now[t]
+                field[t, l] = now[t]
             return now
 
         carry = lax.fori_loop(0, CHUNK, up, carry)
@@ -273,59 +267,63 @@
 
     lax.fori_loop(0, chunks, up_chunk, tuple(inflow[t] for t in range(trac)))
 
-    def unit(i, _):
-        s = i // chunks
-        c = chunks - 1 - lax.rem(i, chunks)
-        field = lax.rem(s, 2)
-
-        @pl.when(s > 0)
-        def _():
-            for copy in edges(s - 1, c):
-                copy.wait_send()
-
-        for copy in edges(s, c):
-            copy.wait_recv()
-
-        def level(k, _):
-            l = c * CHUNK + k
-            keep_l = keep[l]
-            east_l = east[l]
-            west_l = west[l]
-            for t in range(trac):
-                here = q[field, t, l]
-                after = jnp.where(last, from_right[s, c, t, pl.ds(k, 1), :], pltpu.roll(here, width - 1, 0))
-                before = jnp.where(first, from_left[s, c, t, pl.ds(k, 1), :], pltpu.roll(here, 1, 0))
-                q[1 - field, t, l] = (
-                    keep_l * here
-                    + east_l * after
-                    + west_l * before
-                    + north * pltpu.roll(here, rows - 1, 1)
-                    + south * pltpu.roll(here, 1, 1)
-                )
+    def step(s):
+        source, target = fields[s % 2], fields[(s + 1) % 2]
+
+        def unit(i, _):
+            c = chunks - 1 - i
+            if s > 0:
+                for copy in edges(s - 1, c):
+                    copy.wait_send()
+            for copy in edges(s, c):
+                copy.wait_recv()
+
+            def level(k, _):
+                l = c * CHUNK + k
+                keep_l = keep[l]
+                east_l = east[l]
+                west_l = west[l]
+                for t in range(trac):
+                    here = source[t, l]
+                    after = jnp.where(last, from_right[s, c, t, pl.ds(k, 1), :], pltpu.roll(here, width - 1, 0))
+                    before = jnp.where(first, from_left[s, c, t, pl.ds(k, 1), :], pltpu.roll(here, 1, 0))
+                    target[t, l] = (
+                        keep_l * here
+                        + east_l * after
+                        + west_l * before
+                        + north * pltpu.roll(here, rows - 1, 1)
+                        + south * pltpu.roll(here, 1, 1)
+                    )
+                return 0
+
+            lax.fori_loop(0, CHUNK, level, 0, unroll=True)
+            if s < STEPS - 1:
+                for copy in edges(s + 1, c):
+                    copy.start()
             return 0
 
-        lax.fori_loop(0, CHUNK, level, 0)
-
-        @pl.when(s < STEPS - 1)
-        def _():
-            for copy in edges(s + 1, c):
-                copy.start()
-
-        @pl.when(s == STEPS - 1)
-        def _():
-            chunk_store(c).start()
-
-        return 0
-
-    lax.fori_loop(0, STEPS * chunks, unit, 0)
+        lax.fori_loop(0, chunks, unit, 0)
+
+    for s in range(STEPS):
+        step(s)
 
     for c in range(chunks):
         for copy in edges(STEPS - 1, c):
             copy.wait_send()
-        chunk_store(c).wait()
     for copy in early + exchange:
         copy.wait_send()
-    store_inflow.wait()
+
+
+def write_back(value, inflow, value_out, inflow_out, sem):
+    levels = value.shape[2] // 4
+    copies = [pltpu.make_async_copy(inflow, inflow_out, sem.at[4])]
+    for i in range(4):
+        part = pl.ds(i * levels, levels)
+        copies.append(pltpu.make_async_copy(value.at[:, :, part], value_out.at[:, :, part], sem.at[i]))
+    for copy in copies:
+        copy.start()
+    for copy in copies:
+        copy.wait()
 
 
 def per_device(count, tracers, diffusivity, conductance, face_velocity, partner, weight, sea_mask):
@@ -333,20 +331,22 @@
     chunks = lev // CHUNK
     full = (lev, width, rows)
     flat = (width, rows)
-    anywhere = pl.BlockSpec(memory_space=pl.ANY)
+    anywhere = pl.BlockSpec(memory_space=pltpu.HBM)
     edge = (STEPS, chunks, trac, CHUNK, rows)
     dma = pltpu.SemaphoreType.DMA
     real = jnp.float32
-    return pl.pallas_call(
+    shapes = (
+        jax.ShapeDtypeStruct(tracers.shape, real),
+        jax.ShapeDtypeStruct((1, trac, width, rows), real),
+    )
+    vmem = pl.BlockSpec(memory_space=pltpu.VMEM)
+    results = pl.pallas_call(
         functools.partial(kernel, count),
-        out_shape=(
-            jax.ShapeDtypeStruct(tracers.shape, real),
-            jax.ShapeDtypeStruct((1, trac, width, rows), real),
-        ),
+        out_shape=shapes,
         in_specs=[anywhere] * 7,
-        out_specs=(anywhere, anywhere),
+        out_specs=(vmem, vmem),
         scratch_shapes=[
-            pltpu.VMEM((2, trac) + full, real),
+            pltpu.VMEM((trac,) + full, real),
             pltpu.VMEM(full, real),
             pltpu.VMEM(full, real),
             pltpu.VMEM(full, real),
@@ -364,9 +364,7 @@
             pltpu.VMEM((trac + 2, 3 * width, rows), real),
             pltpu.VMEM((2,) + flat, jnp.int32),
             pltpu.VMEM((2,) + flat, jnp.int32),
-            pltpu.VMEM((trac,) + flat, real),
             dma((6,)),
-            dma((chunks,)),
             dma((chunks,)),
             dma((8,)),
             dma((8,)),
@@ -374,10 +372,19 @@
             dma((2, STEPS, chunks)),
         ],
         compiler_params=pltpu.CompilerParams(
-            collective_id=0, has_side_effects=True, vmem_limit_bytes=56 * 1024 * 1024
+            collective_id=0, has_side_effects=True, vmem_limit_bytes=34 * 1024 * 1024
         ),
         name="coupled_step",
-    )(tracers, diffusivity, conductance, face_velocity, partner, weight, sea_mask)
+    )(*[pltpu.with_memory_space_constraint(a, pltpu.HBM) for a in (tracers, diffusivity, conductance, face_velocity, partner, weight, sea_mask)])
+    return pl.pallas_call(
+        write_back,
+        out_shape=shapes,
+        in_specs=[vmem, vmem],
+        out_specs=(anywhere, anywhere),
+        scratch_shapes=[dma((5,))],
+        compiler_params=pltpu.CompilerParams(vmem_limit_bytes=1024 * 1024),
+        name="write_back",
+    )(*results)
 
 
 def solution(mesh):

time: 129 us -> 75.9 us (0.59)
  Pallas kernels: 119 us -> 74.5 us
  local copies, waits for them, and re-layouts: 9.39 us -> 0 us
    pallas_call x1 -> x2, Pallas kernels: 119 us -> 74.5 us  [the longest x1 71.1 us: per_device(): pl.pallas_call(functools.partial(kernel, count), out_shape=shapes, in_spe...]
    unnamed x4 -> x0, local copies, waits for them, and re-layouts: 9.39 us -> none
where the time goes in v1:
time: 75.9 us; the launch traced here: 75.1 us
  Pallas kernels  74.5 us (98%)
    pallas_call x1, Pallas kernels, per_device(): pl.pallas_call(functools.partial(kernel, count), out_shape=shapes, in_spe...  71.1 us
    pallas_call x1, Pallas kernels, per_device(): pl.pallas_call(write_back, out_shape=shapes, in_specs=[vmem, vmem], out_s...  3.42 us

profile of v1, /device:TPU:0, one launch (start us, length us, event | category | flops | bytes accessed | tf_op | source)
XLA Modules:
  0.0 75.1 jit_solution(5389969674399011070)
XLA Ops:
  0.6 71.1 %coupled_step.1 = (f32[1,4,64,16,512]{4,3,2,1,0:T(8,128)S(1)}, f32[1,4,16,512]{3,2,1,0:T(8,128)S(1)}) custom-call(f32[1,4,64,16,512]{4,3,2,1,0:T(8,128)} %tracers.1, f32[1,63,16,512]{3,2,1,0:T(8,128)} %diffusivity.1, f32[1,16,512]{2,1,0:T(8,128)} %conductance.1, f32[1,64,16,512]{3,2,1,0:T(8,128)} %velocity.1, s32[1,2,16,512]{3,2,1,0:T(8,128)} %partner.1, ...), custom_call_target="tpu_custom_call" | custom-call | tf_op jit(solution)/shard_map/coupled_step/pallas_call | solution.py:343
  71.7 3.4 %write_back.1 = (f32[1,4,64,16,512]{4,3,2,1,0:T(8,128)}, f32[1,4,16,512]{3,2,1,0:T(8,128)}) custom-call(f32[1,4,64,16,512]{4,3,2,1,0:T(8,128)S(1)} %get-tuple-element.4.value, f32[1,4,16,512]{3,2,1,0:T(8,128)S(1)} %get-tuple-element.5.inflow), custom_call_target="tpu_custom_call" | custom-call | tf_op jit(solution)/shard_map/write_back/pallas_call | solution.py:379

commit v2 on v1

--- a/solution.py
+++ b/solution.py
@@ -11,6 +11,7 @@
 QUANT = 16
 CHUNK = 8
 REACH = 9
+EARLY = 4
 
 diffusion_nu = 0.12
 MESH = pl.DeviceIdType.MESH
@@ -45,12 +46,17 @@
     wide,
     partner_own,
     weight_own,
+    response,
+    response_edge,
+    inflow_edge,
     load_sem,
     tracer_sem,
     misc_send,
     misc_recv,
     edge_send,
     edge_recv,
+    reply_send,
+    reply_recv,
 ):
     _, trac, lev, width, rows = out.shape
     field = out.at[0]
@@ -84,8 +90,7 @@
     loads[0].start()
     for c in range(chunks):
         chunk_load(c).start()
-    for load in loads[1:]:
-        load.start()
+    loads[1].start()
 
     barrier = pltpu.get_barrier_semaphore()
     peers = [(component, left), (component, right), (other, tile), (other, left), (other, right)]
@@ -108,21 +113,33 @@
         send(1, sea_mask.at[pl.ds(half, half)], mask_left, (component, right)),
         send(2, sea_mask.at[pl.ds(0, half)], mask_right, (component, left)),
     ]
-    exchange = [
-        send(3, terms, wide.at[:, pl.ds(width, width)], (other, tile)),
-        send(4, terms.at[:, pl.ds(half, half)], wide.at[:, pl.ds(half, half)], (other, right)),
-        send(5, terms.at[:, half - 1], wide.at[:, half - 1], (other, right)),
-        send(6, terms.at[:, pl.ds(0, half)], wide.at[:, pl.ds(2 * width, half)], (other, left)),
-        send(7, terms.at[:, half], wide.at[:, 2 * width + half], (other, left)),
-    ]
+
+    def exchange_of(base, begin, size):
+        ch = pl.ds(begin, size)
+        moves = [
+            (pl.ds(0, width), pl.ds(width, width), tile),
+            (pl.ds(half, half), pl.ds(half, half), right),
+            (half - 1, half - 1, right),
+            (pl.ds(0, half), pl.ds(2 * width, half), left),
+            (half, 2 * width + half, left),
+        ]
+        return [
+            send(base + i, terms.at[ch, mine], wide.at[ch, theirs], (other, peer))
+            for i, (mine, theirs, peer) in enumerate(moves)
+        ]
+
+    exchange_late = exchange_of(3, 0, trac)
+    exchange_early = exchange_of(8, trac, 2)
+    exchange = exchange_late + exchange_early
     for copy in early:
         copy.start()
 
-    def edges(s, c):
+    def edges(s, c, source=None):
         part = pl.ds(c * CHUNK, CHUNK)
+        source = fields[s % 2] if source is None else source
         return [
             pltpu.make_async_remote_copy(
-                src_ref=fields[s % 2].at[:, part, column],
+                src_ref=source.at[:, part, column],
                 dst_ref=target.at[s, c],
                 send_sem=edge_send.at[side, s, c],
                 recv_sem=edge_recv.at[side, s, c],
@@ -134,6 +151,26 @@
             )
         ]
 
+    sides = [(width - 1, right), (0, left)]
+
+    def replies(i):
+        return [
+            pltpu.make_async_remote_copy(
+                src_ref=response.at[i, :, column],
+                dst_ref=response_edge.at[side, i],
+                send_sem=reply_send.at[side, i],
+                recv_sem=reply_recv.at[side, i],
+                device_id=(component, peer),
+                device_id_type=MESH,
+            )
+            for side, (column, peer) in enumerate(sides)
+        ]
+
+    inflow_sends = [
+        send(13 + side, inflow.at[:, column], inflow_edge.at[side], (component, peer))
+        for side, (column, peer) in enumerate(sides)
+    ]
+
     loads[0].wait()
     zero = jnp.zeros((width, rows), jnp.float32)
     lower[lev - 1] = zero
@@ -151,6 +188,10 @@
     lax.fori_loop(0, lev, factor, (zero, zero))
     slope = inverse[lev - 1]
     ratio[lev - 1] = slope
+    terms[trac] = slope
+    loads[1].wait()
+    for copy in exchange_early:
+        copy.start()
 
     def down_chunk(c, carry):
         chunk_load(c).wait()
@@ -169,10 +210,30 @@
     finals = lax.fori_loop(0, chunks, down_chunk, (zero,) * trac)
     for t in range(trac):
         terms[t] = finals[t]
-    terms[trac] = slope
-    loads[1].wait()
-    for copy in exchange:
+    for copy in exchange_late:
         copy.start()
+    for load in loads[2:]:
+        load.start()
+
+    def early_chunk(i, carry):
+        c = chunks - 1 - i
+
+        def up(k, above):
+            l = c * CHUNK + CHUNK - 1 - k
+            slant = ratio[l]
+            now = tuple(field[t, l] + slant * above[t] for t in range(trac))
+            for t in range(trac):
+                spare[t, l] = now[t]
+            reply = slant * above[trac]
+            response[i, CHUNK - 1 - k] = reply
+            return now + (reply,)
+
+        carry = lax.fori_loop(0, CHUNK, up, carry, unroll=True)
+        for copy in edges(0, c, spare) + replies(i):
+            copy.start()
+        return carry
+
+    lax.fori_loop(0, EARLY, early_chunk, (zero,) * trac + (jnp.ones((width, rows), jnp.float32),))
 
     for load in loads[2:]:
         load.wait()
@@ -249,6 +310,9 @@
 
     lax.fori_loop(0, rows // lanes, surface, 0)
 
+    for copy in inflow_sends:
+        copy.start()
+
     def up_chunk(i, carry):
         c = chunks - 1 - i
 
@@ -261,8 +325,12 @@
             return now
 
         carry = lax.fori_loop(0, CHUNK, up, carry)
-        for copy in edges(0, c):
-            copy.start()
+
+        @pl.when(i >= EARLY)
+        def _():
+            for copy in edges(0, c):
+                copy.start()
+
         return carry
 
     lax.fori_loop(0, chunks, up_chunk, tuple(inflow[t] for t in range(trac)))
@@ -272,11 +340,35 @@
 
         def unit(i, _):
             c = chunks - 1 - i
-            if s > 0:
+            if s == 1:
+
+                @pl.when(i >= EARLY)
+                def _():
+                    for copy in edges(0, c):
+                        copy.wait_send()
+
+            if s > 1:
                 for copy in edges(s - 1, c):
                     copy.wait_send()
             for copy in edges(s, c):
                 copy.wait_recv()
+            if s == 0:
+
+                @pl.when(i == 0)
+                def _():
+                    for copy in inflow_sends:
+                        copy.wait_recv()
+
+                @pl.when(i < EARLY)
+                def _():
+                    for copy in edges(0, c, spare) + replies(i):
+                        copy.wait_send()
+                    for copy in replies(i):
+                        copy.wait_recv()
+                    for side, edge in enumerate((from_left, from_right)):
+                        for t in range(trac):
+                            edge[0, c, t] = edge[0, c, t] + response_edge[side, i] * inflow_edge[side, pl.ds(t, 1), :]
+
 
             def level(k, _):
                 l = c * CHUNK + k
@@ -310,7 +402,7 @@
     for c in range(chunks):
         for copy in edges(STEPS - 1, c):
             copy.wait_send()
-    for copy in early + exchange:
+    for copy in early + exchange + inflow_sends:
         copy.wait_send()
 
 
@@ -364,12 +456,17 @@
             pltpu.VMEM((trac + 2, 3 * width, rows), real),
             pltpu.VMEM((2,) + flat, jnp.int32),
             pltpu.VMEM((2,) + flat, jnp.int32),
+            pltpu.VMEM((EARLY, CHUNK) + flat, real),
+            pltpu.VMEM((2, EARLY, CHUNK, rows), real),
+            pltpu.VMEM((2, trac, rows), real),
             dma((6,)),
             dma((chunks,)),
-            dma((8,)),
-            dma((8,)),
+            dma((15,)),
+            dma((15,)),
             dma((2, STEPS, chunks)),
             dma((2, STEPS, chunks)),
+            dma((2, EARLY)),
+            dma((2, EARLY)),
         ],
         compiler_params=pltpu.CompilerParams(
             collective_id=0, has_side_effects=True, vmem_limit_bytes=34 * 1024 * 1024

time: 75.9 us -> 70.4 us (0.928)
  Pallas kernels: 74.5 us -> 69.6 us
    pallas_call x1, Pallas kernels: 71.1 us -> 66.2 us  [per_device(): pl.pallas_call(functools.partial(kernel, count), out_shape=shapes, in_spe...]
where the time goes in v2:
time: 70.4 us; the launch traced here: 70.2 us
  Pallas kernels  69.6 us (99%)
    pallas_call x1, Pallas kernels, per_device(): pl.pallas_call(functools.partial(kernel, count), out_shape=shapes, in_spe...  66.2 us
    pallas_call x1, Pallas kernels, per_device(): pl.pallas_call(write_back, out_shape=shapes, in_specs=[vmem, vmem], out_s...  3.42 us

profile of v2, /device:TPU:0, one launch (start us, length us, event | category | flops | bytes accessed | tf_op | source)
XLA Modules:
  0.0 70.2 jit_solution(2709361944774145308)
XLA Ops:
  0.6 66.2 %coupled_step.1 = (f32[1,4,64,16,512]{4,3,2,1,0:T(8,128)S(1)}, f32[1,4,16,512]{3,2,1,0:T(8,128)S(1)}) custom-call(f32[1,4,64,16,512]{4,3,2,1,0:T(8,128)} %tracers.1, f32[1,63,16,512]{3,2,1,0:T(8,128)} %diffusivity.1, f32[1,16,512]{2,1,0:T(8,128)} %conductance.1, f32[1,64,16,512]{3,2,1,0:T(8,128)} %velocity.1, s32[1,2,16,512]{3,2,1,0:T(8,128)} %partner.1, ...), custom_call_target="tpu_custom_call" | custom-call | tf_op jit(solution)/shard_map/coupled_step/pallas_call | solution.py:435
  66.8 3.4 %write_back.1 = (f32[1,4,64,16,512]{4,3,2,1,0:T(8,128)}, f32[1,4,16,512]{3,2,1,0:T(8,128)}) custom-call(f32[1,4,64,16,512]{4,3,2,1,0:T(8,128)S(1)} %get-tuple-element.4.value, f32[1,4,16,512]{3,2,1,0:T(8,128)S(1)} %get-tuple-element.5.inflow), custom_call_target="tpu_custom_call" | custom-call | tf_op jit(solution)/shard_map/write_back/pallas_call | solution.py:476

commit v3 on v2

--- a/solution.py
+++ b/solution.py
@@ -90,7 +90,8 @@
     loads[0].start()
     for c in range(chunks):
         chunk_load(c).start()
-    loads[1].start()
+    for load in loads[1:]:
+        load.start()
 
     barrier = pltpu.get_barrier_semaphore()
     peers = [(component, left), (component, right), (other, tile), (other, left), (other, right)]
@@ -185,7 +186,7 @@
         ratio[l] = ratio_now
         return high, ratio_now
 
-    lax.fori_loop(0, lev, factor, (zero, zero))
+    lax.fori_loop(0, lev, factor, (zero, zero), unroll=4)
     slope = inverse[lev - 1]
     ratio[lev - 1] = slope
     terms[trac] = slope
@@ -205,15 +206,13 @@
                 field[t, l] = now[t]
             return now
 
-        return lax.fori_loop(0, CHUNK, down, carry)
+        return lax.fori_loop(0, CHUNK, down, carry, unroll=4)
 
     finals = lax.fori_loop(0, chunks, down_chunk, (zero,) * trac)
     for t in range(trac):
         terms[t] = finals[t]
     for copy in exchange_late:
         copy.start()
-    for load in loads[2:]:
-        load.start()
 
     def early_chunk(i, carry):
         c = chunks - 1 - i

time: 70.4 us -> 69.5 us (0.987)
  Pallas kernels: 69.6 us -> 68.8 us
    pallas_call x1, Pallas kernels: 66.2 us -> 65.4 us  [per_device(): pl.pallas_call(functools.partial(kernel, count), out_shape=shapes, in_spe...]
where the time goes in v3:
time: 69.5 us; the launch traced here: 69.4 us
  Pallas kernels  68.8 us (99%)
    pallas_call x1, Pallas kernels, per_device(): pl.pallas_call(functools.partial(kernel, count), out_shape=shapes, in_spe...  65.4 us
    pallas_call x1, Pallas kernels, per_device(): pl.pallas_call(write_back, out_shape=shapes, in_specs=[vmem, vmem], out_s...  3.42 us

profile of v3, /device:TPU:0, one launch (start us, length us, event | category | flops | bytes accessed | tf_op | source)
XLA Modules:
  0.0 69.4 jit_solution(15360474243214684981)
XLA Ops:
  0.6 65.4 %coupled_step.1 = (f32[1,4,64,16,512]{4,3,2,1,0:T(8,128)S(1)}, f32[1,4,16,512]{3,2,1,0:T(8,128)S(1)}) custom-call(f32[1,4,64,16,512]{4,3,2,1,0:T(8,128)} %tracers.1, f32[1,63,16,512]{3,2,1,0:T(8,128)} %diffusivity.1, f32[1,16,512]{2,1,0:T(8,128)} %conductance.1, f32[1,64,16,512]{3,2,1,0:T(8,128)} %velocity.1, s32[1,2,16,512]{3,2,1,0:T(8,128)} %partner.1, ...), custom_call_target="tpu_custom_call" | custom-call | tf_op jit(solution)/shard_map/coupled_step/pallas_call | solution.py:434
  66.0 3.4 %write_back.1 = (f32[1,4,64,16,512]{4,3,2,1,0:T(8,128)}, f32[1,4,16,512]{3,2,1,0:T(8,128)}) custom-call(f32[1,4,64,16,512]{4,3,2,1,0:T(8,128)S(1)} %get-tuple-element.4.value, f32[1,4,16,512]{3,2,1,0:T(8,128)S(1)} %get-tuple-element.5.inflow), custom_call_target="tpu_custom_call" | custom-call | tf_op jit(solution)/shard_map/write_back/pallas_call | solution.py:475

commit v4 on v3

--- a/solution.py
+++ b/solution.py
@@ -268,7 +268,7 @@
         west[l] = open_west * (jnp.maximum(before, 0.0) + diffusion_nu)
         return 0
 
-    lax.fori_loop(0, lev, coefficients, 0)
+    lax.fori_loop(0, lev, coefficients, 0, unroll=2)
 
     for copy in exchange:
         copy.wait_recv()
@@ -323,7 +323,7 @@
                 field[t, l] = now[t]
             return now
 
-        carry = lax.fori_loop(0, CHUNK, up, carry)
+        carry = lax.fori_loop(0, CHUNK, up, carry, unroll=True)
 
         @pl.when(i >= EARLY)
         def _():

time: 69.5 us -> 69.5 us (level)
  no operation moved by 1% of the time
where the time goes in v4:
time: 69.5 us; the launch traced here: 69.4 us
  Pallas kernels  68.8 us (99%)
    pallas_call x1, Pallas kernels, per_device(): pl.pallas_call(functools.partial(kernel, count), out_shape=shapes, in_spe...  65.4 us
    pallas_call x1, Pallas kernels, per_device(): pl.pallas_call(write_back, out_shape=shapes, in_specs=[vmem, vmem], out_s...  3.42 us

profile of v4, /device:TPU:0, one launch (start us, length us, event | category | flops | bytes accessed | tf_op | source)
XLA Modules:
  0.0 69.4 jit_solution(3970553581229624510)
XLA Ops:
  0.6 65.4 %coupled_step.1 = (f32[1,4,64,16,512]{4,3,2,1,0:T(8,128)S(1)}, f32[1,4,16,512]{3,2,1,0:T(8,128)S(1)}) custom-call(f32[1,4,64,16,512]{4,3,2,1,0:T(8,128)} %tracers.1, f32[1,63,16,512]{3,2,1,0:T(8,128)} %diffusivity.1, f32[1,16,512]{2,1,0:T(8,128)} %conductance.1, f32[1,64,16,512]{3,2,1,0:T(8,128)} %velocity.1, s32[1,2,16,512]{3,2,1,0:T(8,128)} %partner.1, ...), custom_call_target="tpu_custom_call" | custom-call | tf_op jit(solution)/shard_map/coupled_step/pallas_call | solution.py:434
  66.0 3.4 %write_back.1 = (f32[1,4,64,16,512]{4,3,2,1,0:T(8,128)}, f32[1,4,16,512]{3,2,1,0:T(8,128)}) custom-call(f32[1,4,64,16,512]{4,3,2,1,0:T(8,128)S(1)} %get-tuple-element.4.value, f32[1,4,16,512]{3,2,1,0:T(8,128)S(1)} %get-tuple-element.5.inflow), custom_call_target="tpu_custom_call" | custom-call | tf_op jit(solution)/shard_map/write_back/pallas_call | solution.py:475

commit v5 on v3

--- a/solution.py
+++ b/solution.py
@@ -236,40 +236,6 @@
 
     for load in loads[2:]:
         load.wait()
-    for copy in early:
-        copy.wait_recv()
-    row = lax.broadcasted_iota(jnp.int32, (width, rows), 0)
-    lane = lax.broadcasted_iota(jnp.int32, (width, rows), 1)
-    first = row == 0
-    last = row == width - 1
-
-    def openness_of(mask):
-        return jnp.where(component == 1, mask.astype(jnp.float32), jnp.ones(mask.shape, jnp.float32))
-
-    openness = openness_of(mask_own[...])
-    open_right = openness_of(mask_right[pl.ds(0, 1), :])
-    open_left = openness_of(mask_left[pl.ds(half - 1, 1), :])
-    open_east = openness * jnp.where(last, open_right, pltpu.roll(openness, width - 1, 0))
-    open_west = openness * jnp.where(first, open_left, pltpu.roll(openness, 1, 0))
-    north = jnp.where(lane == rows - 1, 0.0, diffusion_nu * openness * pltpu.roll(openness, rows - 1, 1))
-    south = jnp.where(lane == 0, 0.0, diffusion_nu * openness * pltpu.roll(openness, 1, 1))
-
-    def coefficients(l, _):
-        here = speed[l]
-        before = jnp.where(first, speed_left[pl.ds(l, 1), :], pltpu.roll(here, 1, 0))
-        keep[l] = (
-            1.0
-            - north
-            - south
-            - open_east * (jnp.maximum(here, 0.0) + diffusion_nu)
-            + open_west * (jnp.minimum(before, 0.0) - diffusion_nu)
-        )
-        east[l] = open_east * (diffusion_nu - jnp.minimum(here, 0.0))
-        west[l] = open_west * (jnp.maximum(before, 0.0) + diffusion_nu)
-        return 0
-
-    lax.fori_loop(0, lev, coefficients, 0)
-
     for copy in exchange:
         copy.wait_recv()
     columns = count * width
@@ -333,6 +299,40 @@
         return carry
 
     lax.fori_loop(0, chunks, up_chunk, tuple(inflow[t] for t in range(trac)))
+
+    for copy in early:
+        copy.wait_recv()
+    row = lax.broadcasted_iota(jnp.int32, (width, rows), 0)
+    lane = lax.broadcasted_iota(jnp.int32, (width, rows), 1)
+    first = row == 0
+    last = row == width - 1
+
+    def openness_of(mask):
+        return jnp.where(component == 1, mask.astype(jnp.float32), jnp.ones(mask.shape, jnp.float32))
+
+    openness = openness_of(mask_own[...])
+    open_right = openness_of(mask_right[pl.ds(0, 1), :])
+    open_left = openness_of(mask_left[pl.ds(half - 1, 1), :])
+    open_east = openness * jnp.where(last, open_right, pltpu.roll(openness, width - 1, 0))
+    open_west = openness * jnp.where(first, open_left, pltpu.roll(openness, 1, 0))
+    north = jnp.where(lane == rows - 1, 0.0, diffusion_nu * openness * pltpu.roll(openness, rows - 1, 1))
+    south = jnp.where(lane == 0, 0.0, diffusion_nu * openness * pltpu.roll(openness, 1, 1))
+
+    def coefficients(l, _):
+        here = speed[l]
+        before = jnp.where(first, speed_left[pl.ds(l, 1), :], pltpu.roll(here, 1, 0))
+        keep[l] = (
+            1.0
+            - north
+            - south
+            - open_east * (jnp.maximum(here, 0.0) + diffusion_nu)
+            + open_west * (jnp.minimum(before, 0.0) - diffusion_nu)
+        )
+        east[l] = open_east * (diffusion_nu - jnp.minimum(here, 0.0))
+        west[l] = open_west * (jnp.maximum(before, 0.0) + diffusion_nu)
+        return 0
+
+    lax.fori_loop(0, lev, coefficients, 0)
 
     def step(s):
         source, target = fields[s % 2], fields[(s + 1) % 2]

time: 69.5 us -> 69.5 us (level)
  no operation moved by 1% of the time
where the time goes in v5:
time: 69.5 us; the launch traced here: 69.4 us
  Pallas kernels  68.8 us (99%)
    pallas_call x1, Pallas kernels, per_device(): pl.pallas_call(functools.partial(kernel, count), out_shape=shapes, in_spe...  65.4 us
    pallas_call x1, Pallas kernels, per_device(): pl.pallas_call(write_back, out_shape=shapes, in_specs=[vmem, vmem], out_s...  3.42 us

profile of v5, /device:TPU:0, one launch (start us, length us, event | category | flops | bytes accessed | tf_op | source)
XLA Modules:
  0.0 69.4 jit_solution(3362876335356454768)
XLA Ops:
  0.6 65.4 %coupled_step.1 = (f32[1,4,64,16,512]{4,3,2,1,0:T(8,128)S(1)}, f32[1,4,16,512]{3,2,1,0:T(8,128)S(1)}) custom-call(f32[1,4,64,16,512]{4,3,2,1,0:T(8,128)} %tracers.1, f32[1,63,16,512]{3,2,1,0:T(8,128)} %diffusivity.1, f32[1,16,512]{2,1,0:T(8,128)} %conductance.1, f32[1,64,16,512]{3,2,1,0:T(8,128)} %velocity.1, s32[1,2,16,512]{3,2,1,0:T(8,128)} %partner.1, ...), custom_call_target="tpu_custom_call" | custom-call | tf_op jit(solution)/shard_map/coupled_step/pallas_call | solution.py:434
  66.0 3.4 %write_back.1 = (f32[1,4,64,16,512]{4,3,2,1,0:T(8,128)}, f32[1,4,16,512]{3,2,1,0:T(8,128)}) custom-call(f32[1,4,64,16,512]{4,3,2,1,0:T(8,128)S(1)} %get-tuple-element.4.value, f32[1,4,16,512]{3,2,1,0:T(8,128)S(1)} %get-tuple-element.5.inflow), custom_call_target="tpu_custom_call" | custom-call | tf_op jit(solution)/shard_map/write_back/pallas_call | solution.py:475
